TPU v7x, 256 devices: a whole 4x4x8 slice. The times are simulated.
256 devices in a mesh: dp: 32 (over z, x), grp: 8 (over y, core).
Axes of the slice: x: 4, y: 4, z: 8, core: 2. Of those that a mesh axis runs over, the one named last changes fastest.
Arguments:
- grad: bfloat16 [16, 2048, 2048], P(None, 'dp'), may hold values from -81 to 81
Outputs:
- update: bfloat16 [32, 1024, 2048], P('dp', 'grp')
All inputs are finite; a program needn't handle non-finite values.
Results may differ from a plain program's by a relative error of at most 0.0033.
The roundings to bfloat16 on the way count: a program that leaves them out, or rounds other values in their place, can miss the bound.
Values may be sent and summed in bfloat16 or wider, within the bound.
A program may use at most 128 MiB of HBM per device.

v0:
```python
import math

import jax
import jax.numpy as jnp
from jax import lax
from jax.sharding import PartitionSpec as P

PSTEPS = 8


damping = 0.1
graft_floor = 1e-06


def from_partner(value, axis, distance):
    mask = 2**distance
    pairs = [(source, source ^ mask) for source in range(lax.axis_size(axis))]
    return lax.ppermute(value, axis, pairs)


def per_device(grad):
    side = lax.axis_index("dp") % 2
    owned = lax.axis_index("dp") // 2
    nblocks = grad.shape[0]
    width = grad.shape[2]
    sent = jnp.repeat(grad, 2, axis=0)
    whole = lax.all_to_all(sent, "dp", split_axis=0, concat_axis=1, tiled=True)[0]
    row_count = width // lax.axis_size("grp")
    first = lax.axis_index("grp") * row_count
    operand = jnp.where(side == 0, whole, whole.T)
    own_rows = lax.dynamic_slice_in_dim(operand, first, row_count, 0)
    eye_rows = (
        first + lax.broadcasted_iota(jnp.int32, (row_count, width), 0)
        == lax.broadcasted_iota(jnp.int32, (row_count, width), 1)
    ).astype(jnp.float32)
    stat = (
        lax.dot_general(
            own_rows, operand, (((1,), (1,)), ((), ())), preferred_element_type=jnp.float32
        )
        / width
        + damping * eye_rows
    )
    vector = jnp.ones((width,), jnp.float32) / math.sqrt(width)
    norm = jnp.float32(1.0)
    for step in range(PSTEPS):
        piece = jnp.dot(stat, vector, precision=lax.Precision.HIGHEST)
        image = lax.all_gather(piece, "grp", axis=0, tiled=True)
        norm = jnp.sqrt(jnp.sum(image * image))
        vector = image / norm
    t_zero = ((5.0 * eye_rows - stat / norm) / 4.0).astype(jnp.bfloat16)
    t_full = lax.all_gather(t_zero, "grp", axis=0, tiled=True)
    square = jnp.dot(t_zero, t_full, preferred_element_type=jnp.float32).astype(jnp.bfloat16)
    columns = square
    fourth = jnp.dot(
        columns,
        lax.all_gather(square, "grp", axis=0, tiled=True),
        preferred_element_type=jnp.float32,
    )
    fifth = jnp.dot(fourth.astype(jnp.bfloat16), t_full, preferred_element_type=jnp.float32)
    moved = 5.0 * fourth - 4.0 * fifth
    t_one = ((5.0 * eye_rows - moved) / 4.0).astype(jnp.bfloat16)
    root = jnp.dot(t_one, t_full, preferred_element_type=jnp.float32).astype(jnp.bfloat16)
    partner = from_partner(root, "dp", 0)
    left_rows = jnp.where(side == 0, root, partner)
    right_rows = jnp.where(side == 0, partner, root)
    half_rows = row_count // 2
    left_half = lax.dynamic_slice_in_dim(left_rows, side * half_rows, half_rows, 0)
    mixed = jnp.dot(left_half, whole, preferred_element_type=jnp.float32).astype(jnp.bfloat16)
    columns = mixed
    result = jnp.dot(
        columns,
        lax.all_gather(right_rows, "grp", axis=0, tiled=True),
        preferred_element_type=jnp.float32,
    )
    grad_rows = lax.dynamic_slice_in_dim(whole, first + side * half_rows, half_rows, 0).astype(
        jnp.float32
    )
    grad_sq = jnp.sum(grad_rows * grad_rows)
    upd_sq = jnp.sum(result * result)
    onehot = (jnp.arange(nblocks) == owned).astype(jnp.float32)
    grad_tot, upd_tot = lax.psum((onehot * grad_sq, onehot * upd_sq), ("dp", "grp"))
    grad_sum = jnp.sum(grad_tot * onehot)
    upd_sum = jnp.sum(upd_tot * onehot)
    total = width * width
    scaled = result * jnp.sqrt(grad_sum / total) * lax.rsqrt(upd_sum / total + graft_floor)
    return scaled.astype(jnp.bfloat16)[None]


def solution(mesh):
    return jax.shard_map(
        per_device,
        mesh=mesh,
        in_specs=(P(None, "dp", None),),
        out_specs=P("dp", "grp", None),
        check_vma=False,
    )
```

profile of v0, /device:TPU:1, one launch (start us, length us, event | category | flops | bytes accessed | tf_op | source)
XLA Modules:
  0.0 644.2 jit_solution(8392267815496740973)
XLA Ops:
  6.5 6.7 %broadcast_in_dim.6 = bf16[16,2,64,2048]{3,2,1,0:T(8,128)(2,1)} broadcast(bf16[16,64,2048]{2,1,0:T(8,128)(2,1)} %param.1), dimensions={0,2,3} | broadcast | bytes 12582912 | tf_op jit(solution)/shard_map/broadcast_in_dim | solution.py:26
  13.3 12.0 %all-to-all-start = ((bf16[32,64,2048]{2,1,0:T(8,128)(2,1)}), bf16[32,64,2048]{2,1,0:T(8,128)(2,1)}, u32[]{:S(2)}, u32[]{:S(2)}) async-start(bf16[32,64,2048]{2,1,0:T(8,128)(2,1)} %bitcast.98), calls=%async_computation | async-start | bytes 16777216 | tf_op jit(solution)/shard_map/all_to_all | solution.py:27
  25.4 187.4 %all-to-all-done = bf16[32,64,2048]{2,1,0:T(8,128)(2,1)} async-done(((bf16[32,64,2048]{2,1,0:T(8,128)(2,1)}), bf16[32,64,2048]{2,1,0:T(8,128)(2,1)}, u32[]{:S(2)}, u32[]{:S(2)}) %all-to-all-start) | async-done | bytes 8388640 | tf_op jit(solution)/shard_map/all_to_all | solution.py:27
  212.8 12.3 %copy.5 = bf16[2048,2048]{0,1:T(8,128)(2,1)} copy(bf16[2048,2048]{1,0:T(8,128)(2,1)} %bitcast.1) | data formatting | bytes 16777216 | tf_op jit(solution)/shard_map/squeeze | solution.py:27
  225.1 6.4 bitcast_select_fusion
  231.5 2.4 fusion
  234.0 1.7 convolution_bitcast_fusion.7
  235.7 12.4 %all-gather = f32[8,1,256]{2,1,0:T(1,128)S(1)} all-gather(f32[1,1,256]{2,1,0:T(1,128)S(1)} %convolution_bitcast_fusion.7), channel_id=1, replica_groups=mesh['dp'=32,'grp'=8] {'grp'}, dimensions={0}, use_global_device_ids=true | all-gather | bytes 9216 | tf_op jit(solution)/shard_map/all_gather | solution.py:47
  248.1 0.6 multiply_reduce_fusion.9
  249.4 1.7 convolution_bitcast_fusion.6
  251.1 8.1 %all-gather.1 = f32[8,1,256]{2,1,0:T(1,128)S(1)} all-gather(f32[1,1,256]{2,1,0:T(1,128)S(1)} %convolution_bitcast_fusion.6), channel_id=1, replica_groups=mesh['dp'=32,'grp'=8] {'grp'}, dimensions={0}, use_global_device_ids=true | all-gather | bytes 9216 | tf_op jit(solution)/shard_map/all_gather | solution.py:47
  259.2 0.6 multiply_reduce_fusion.8
  260.6 1.7 convolution_bitcast_fusion.5
  262.3 9.5 %all-gather.2 = f32[8,1,256]{2,1,0:T(1,128)S(1)} all-gather(f32[1,1,256]{2,1,0:T(1,128)S(1)} %convolution_bitcast_fusion.5), channel_id=1, replica_groups=mesh['dp'=32,'grp'=8] {'grp'}, dimensions={0}, use_global_device_ids=true | all-gather | bytes 9216 | tf_op jit(solution)/shard_map/all_gather | solution.py:47
  271.8 0.6 multiply_reduce_fusion.7
  273.1 1.7 convolution_bitcast_fusion.4
  274.8 8.1 %all-gather.3 = f32[8,1,256]{2,1,0:T(1,128)S(1)} all-gather(f32[1,1,256]{2,1,0:T(1,128)S(1)} %convolution_bitcast_fusion.4), channel_id=1, replica_groups=mesh['dp'=32,'grp'=8] {'grp'}, dimensions={0}, use_global_device_ids=true | all-gather | bytes 9216 | tf_op jit(solution)/shard_map/all_gather | solution.py:47
  283.0 0.6 multiply_reduce_fusion.6
  284.3 1.7 convolution_bitcast_fusion.3
  286.0 9.7 %all-gather.4 = f32[8,1,256]{2,1,0:T(1,128)S(1)} all-gather(f32[1,1,256]{2,1,0:T(1,128)S(1)} %convolution_bitcast_fusion.3), channel_id=1, replica_groups=mesh['dp'=32,'grp'=8] {'grp'}, dimensions={0}, use_global_device_ids=true | all-gather | bytes 9216 | tf_op jit(solution)/shard_map/all_gather | solution.py:47
  295.7 0.6 multiply_reduce_fusion.5
  297.0 1.7 convolution_bitcast_fusion.2
  298.7 8.1 %all-gather.5 = f32[8,1,256]{2,1,0:T(1,128)S(1)} all-gather(f32[1,1,256]{2,1,0:T(1,128)S(1)} %convolution_bitcast_fusion.2), channel_id=1, replica_groups=mesh['dp'=32,'grp'=8] {'grp'}, dimensions={0}, use_global_device_ids=true | all-gather | bytes 9216 | tf_op jit(solution)/shard_map/all_gather | solution.py:47
  306.8 0.6 multiply_reduce_fusion.4
  308.2 1.7 convolution_bitcast_fusion.1
  309.9 9.5 %all-gather.6 = f32[8,1,256]{2,1,0:T(1,128)S(1)} all-gather(f32[1,1,256]{2,1,0:T(1,128)S(1)} %convolution_bitcast_fusion.1), channel_id=1, replica_groups=mesh['dp'=32,'grp'=8] {'grp'}, dimensions={0}, use_global_device_ids=true | all-gather | bytes 9216 | tf_op jit(solution)/shard_map/all_gather | solution.py:47
  319.4 0.6 multiply_reduce_fusion.3
  320.7 1.7 convolution_bitcast_fusion
  322.4 8.1 %all-gather.7 = f32[8,1,256]{2,1,0:T(1,128)S(1)} all-gather(f32[1,1,256]{2,1,0:T(1,128)S(1)} %convolution_bitcast_fusion), channel_id=1, replica_groups=mesh['dp'=32,'grp'=8] {'grp'}, dimensions={0}, use_global_device_ids=true | all-gather | bytes 9216 | tf_op jit(solution)/shard_map/all_gather | solution.py:47
  330.6 0.6 multiply_reduce_fusion.2
  331.9 1.5 fusion.5
  333.4 57.7 %all-gather.12.cloned.1.call-done = bf16[2048,2048]{1,0:T(8,128)(2,1)} async-done(((bf16[256,2048]{1,0:T(8,128)(2,1)}), bf16[2048,2048]{1,0:T(8,128)(2,1)}) %all-gather.12.cloned.1.call-update) | async-done | bytes 8388624 | tf_op jit(solution)/shard_map/all_gather | solution.py:51
  391.1 7.0 %convolution_convert_fusion.1 = bf16[256,2048]{1,0:T(8,128)(2,1)} fusion(bf16[256,2048]{1,0:T(8,128)(2,1)} %fusion.5, bf16[2048,2048]{1,0:T(8,128)(2,1)} %all-gather.12.cloned.1.call-done), kind=kOutput, calls=%fused_computation.8 | convolution fusion | flops 2148007936 | bytes 10485760 | tf_op jit(solution)/shard_map/dot_general | solution.py:52
  398.2 0.3 all-gather.16.cloned.1.call-start
  398.4 52.4 %all-gather.14.cloned.1.call-done = bf16[2048,2048]{1,0:T(8,128)(2,1)} async-done(((bf16[256,2048]{1,0:T(8,128)(2,1)}), bf16[2048,2048]{1,0:T(8,128)(2,1)}) %all-gather.14.cloned.1.call-update) | async-done | bytes 8388624 | tf_op jit(solution)/shard_map/all_gather | solution.py:56
  450.8 7.4 %fusion.27 = f32[256,2048]{1,0:T(8,128)} fusion(bf16[256,2048]{1,0:T(8,128)(2,1)} %convolution_convert_fusion.1, bf16[2048,2048]{1,0:T(8,128)(2,1)} %all-gather.14.cloned.1.call-done), kind=kOutput, calls=%fused_computation.63 | convolution fusion | flops 2147483648 | bytes 11534336 | tf_op jit(solution)/shard_map/dot_general | solution.py:54
  458.2 11.9 %convolution_convert_fusion = bf16[256,2048]{1,0:T(8,128)(2,1)S(1)} fusion(bf16[2048,2048]{1,0:T(8,128)(2,1)} %all-gather.12.cloned.1.call-done, f32[256,2048]{1,0:T(8,128)} %fusion.27, s32[256]{0:T(256)S(1)} %iota_add_fusion), kind=kOutput, calls=%fused_computation.7 | convolution fusion | flops 4300210176 | bytes 11535360 | tf_op jit(solution)/shard_map/dot_general | solution.py:62
  470.2 1.3 collective-permute-start
  471.4 23.3 %collective-permute-done = bf16[256,2048]{1,0:T(8,128)(2,1)S(1)} collective-permute-done((bf16[256,2048]{1,0:T(8,128)(2,1)S(1)}, bf16[256,2048]{1,0:T(8,128)(2,1)S(1)}, u32[]{:S(2)}, u32[]{:S(2)}) %collective-permute-start) | collective-permute-done | bytes 1048608 | tf_op jit(solution)/shard_map/ppermute | solution.py:18
  494.8 1.1 broadcast_select_fusion
  495.9 1.9 multiply_reduce_fusion.1
  497.8 0.6 fusion.21
  498.5 50.8 %all-gather.16.cloned.1.call-done = bf16[2048,2048]{1,0:T(8,128)(2,1)} async-done(((bf16[256,2048]{1,0:T(8,128)(2,1)}), bf16[2048,2048]{1,0:T(8,128)(2,1)}) %all-gather.16.cloned.1.call-update) | async-done | bytes 8388624 | tf_op jit(solution)/shard_map/all_gather | solution.py:72
  549.3 8.8 %multiply_reduce_fusion = (f32[]{:T(128)}, f32[128,2048]{1,0:T(8,128)S(1)}) fusion(bf16[2048,2048]{1,0:T(8,128)(2,1)} %all-gather.16.cloned.1.call-done, bf16[2048,2048]{1,0:T(8,128)(2,1)} %bitcast.1, bf16[256,2048]{1,0:T(8,128)(2,1)S(1)} %collective-permute-done, s32[]{:T(128)S(6)} %select_n.46, bf16[256,2048]{1,0:T(8,128)(2,1)S(1)} %convolution_convert_fusion, ...), kind=kOutput, calls=%fused_computation.24 | convolution fusion | flops 2148532224 | bytes 18874376 | tf_op jit(solution)/shard_map/dot_general | solution.py:70
  558.1 0.6 fusion.20
  558.7 75.9 %all-reduce = (f32[16]{0:T(128)S(1)}, f32[16]{0:T(128)S(1)}) all-reduce(f32[16]{0:T(128)S(1)} %fusion.20, f32[16]{0:T(128)S(1)} %fusion.21), channel_id=1, replica_groups=mesh['dp'=32,'grp'=8] {'dp','grp'}, use_global_device_ids=true, to_apply=%region_12.13 | all-reduce | flops 32 | bytes 256 | tf_op jit(solution)/shard_map/psum | solution.py:81
  634.6 0.7 select_reduce_fusion
  636.8 0.9 fusion.11
  (13 shorter events, 0.2 us)
Async XLA Ops:
  13.3 199.5 %all-to-all-start = ((bf16[32,64,2048]{2,1,0:T(8,128)(2,1)}), bf16[32,64,2048]{2,1,0:T(8,128)(2,1)}, u32[]{:S(2)}, u32[]{:S(2)}) async-start(bf16[32,64,2048]{2,1,0:T(8,128)(2,1)} %bitcast.98), calls=%async_computation | async-start | bytes 16777216 | tf_op jit(solution)/shard_map/all_to_all | solution.py:27
  25.3 365.8 %all-gather.12.cloned.1.call-start = ((), (), s32[]{:S(2)}) async-start(), calls=%async_computation.1 | async-start | bytes 9437184 | tf_op jit(solution)/shard_map/all_gather | solution.py:51
  333.4 117.4 %all-gather.14.cloned.1.call-start = ((), (), s32[]{:S(2)}) async-start(), calls=%async_computation.2 | async-start | bytes 9437184 | tf_op jit(solution)/shard_map/all_gather | solution.py:56
  398.2 151.2 %all-gather.16.cloned.1.call-start = ((), (), s32[]{:S(2)}) async-start(), calls=%async_computation.3 | async-start | bytes 9437184 | tf_op jit(solution)/shard_map/all_gather | solution.py:72
  470.2 24.6 %collective-permute-start = (bf16[256,2048]{1,0:T(8,128)(2,1)S(1)}, bf16[256,2048]{1,0:T(8,128)(2,1)S(1)}, u32[]{:S(2)}, u32[]{:S(2)}) collective-permute-start(bf16[256,2048]{1,0:T(8,128)(2,1)S(1)} %convolution_convert_fusion), channel_id=1, source_target_pairs={{0,8},{8,0},{16,24},{24,16},{32,40},{40,32},{48,56},{56,48},{64,72... | collective-permute-start | bytes 3145736 | tf_op jit(solution)/shard_map/ppermute | solution.py:18
Sparse Core Ops, SparseCore 0:
  333.5 57.5 all-gather.11
  398.3 52.4 all-gather.13
  496.0 53.2 all-gather.15
where the time goes:
time: 645 us; the launch traced here: 644 us
  waiting for transfers between devices  372 us (58%)
  blocking collectives  149 us (23%)
  matrix products  51.4 us (8%)
  between operations  20.3 us (3%)
  local copies, waits for them, and re-layouts  19.1 us (3%)
  other arithmetic  18.7 us (3%)
  starting transfers between devices  13.6 us (2%)
    all_to_all x1, waiting for transfers between devices, per_device(): lax.all_to_all(sent, 'dp', split_axis=0, concat_axis=1, tiled=True)[0]  187 us
    psum x1, blocking collectives, per_device(): lax.psum((onehot * grad_sq, onehot * upd_sq), ('dp', 'grp'))  75.9 us
    all_gather x8, blocking collectives, per_device(): image = lax.all_gather(piece, 'grp', axis=0, tiled=True)  73.6 us
    all_gather x1, waiting for transfers between devices, per_device(): t_full = lax.all_gather(t_zero, 'grp', axis=0, tiled=True)  57.7 us
    all_gather x1, waiting for transfers between devices, per_device(): lax.all_gather(square, 'grp', axis=0, tiled=True)  52.4 us
    all_gather x1, waiting for transfers between devices, per_device(): lax.all_gather(right_rows, 'grp', axis=0, tiled=True)  50.8 us
    ppermute x1, waiting for transfers between devices, from_partner(): return lax.ppermute(value, axis, pairs)  23.3 us
    dot_general x8, matrix products, per_device(): piece = jnp.dot(stat, vector, precision=lax.Precision.HIGHEST)  13.8 us
  transfers between devices with their start and end apart: 5, of which 5 were waited for; matrix products, arithmetic and copies ran while one was open for 0% of the time, Pallas kernels for 0%

commit v1 on v0

v1 whole, which is shorter than its diff:
```python
import functools
import math

import jax
import jax.numpy as jnp
from jax import lax
from jax.experimental import pallas as pl
from jax.experimental.pallas import tpu as pltpu
from jax.sharding import PartitionSpec as P

PSTEPS = 8
damping = 0.1
graft_floor = 1e-06

MESH = pl.DeviceIdType.MESH
f32 = jnp.float32
bf16 = jnp.bfloat16
N = 2048
TILE = 256
HALF = 128
LANES = 128
NT = (((1,), (1,)), ((), ()))
ZORDER = (0, 1, 7, 2, 6, 3, 5, 4)


def at(start, size, unit=None):
    return pl.ds(pl.multiple_of(start, unit or size), size)


def spread_kernel(grad, block, local_sem, send1, recv1, send2, recv2):
    dp = lax.axis_index("dp")
    grp = lax.axis_index("grp")
    z, x = dp // 4, lax.rem(dp, 4)
    y, core = grp // 2, lax.rem(grp, 2)
    up = lax.rem(y + 1, 4) * 2 + core
    down = lax.rem(y + 3, 4) * 2 + core
    across = lax.rem(y + 2, 4) * 2 + core
    sibling = grp + 1 - 2 * core

    def flip(g):
        return g + 1 - 2 * core

    barrier = pltpu.get_barrier_semaphore()

    def greet(k, _):
        pl.semaphore_signal(
            barrier, inc=1, device_id={"dp": lax.rem(dp + k, 32)}, device_id_type=MESH
        )
        return 0

    lax.fori_loop(1, 32, greet, 0)
    for g in (up, down, sibling):
        pl.semaphore_signal(barrier, inc=1, device_id={"grp": g}, device_id_type=MESH)
    pl.semaphore_wait(barrier, 34)

    def piece(dz, dx):
        target = lax.rem(z + dz, 8) * 4 + lax.rem(x + dx, 4)
        return pltpu.make_async_remote_copy(
            src_ref=grad.at[target // 2, :, at(grp * TILE, TILE)],
            dst_ref=block.at[at(dp * 64, 64), at(grp * TILE, TILE)],
            send_sem=send1.at[dz * 4 + dx],
            recv_sem=recv1.at[dz * 4 + dx],
            device_id={"dp": target},
            device_id_type=MESH,
        )

    own = pltpu.make_async_copy(
        grad.at[dp // 2, :, at(grp * TILE, TILE)],
        block.at[at(dp * 64, 64), at(grp * TILE, TILE)],
        local_sem,
    )
    own.start()
    for dz in ZORDER:
        for dx in range(4):
            if dz or dx:
                piece(dz, dx).start()

    def relay(q, column, target, slot):
        rows = at(lax.rem(z + 8 - ZORDER[q], 8) * TILE, TILE)
        ref = block.at[rows, at(column * TILE, TILE)]
        return pltpu.make_async_remote_copy(
            src_ref=ref,
            dst_ref=ref,
            send_sem=send2.at[slot, q],
            recv_sem=recv2.at[slot, q],
            device_id={"grp": target},
            device_id_type=MESH,
        )

    started = []

    def go(*args):
        copy = relay(*args)
        copy.start()
        started.append(copy)

    def first(q):
        for dx in range(4):
            if ZORDER[q] or dx:
                piece(ZORDER[q], dx).wait_recv()
            else:
                own.wait()
        go(q, grp, up, 0)
        go(q, grp, down, 1)
        go(q, grp, sibling, 2)

    def second(q):
        relay(q, down, up, 0).wait_recv()
        if q % 2 == 0:
            go(q, down, up, 3)
        relay(q, up, down, 1).wait_recv()
        if q % 2:
            go(q, up, down, 3)
        go(q, down, sibling, 4)
        go(q, up, sibling, 5)

    def third(q):
        relay(q, across, up, 3).wait_recv()
        go(q, across, sibling, 6)

    for q in range(8 + 2):
        if q < 8:
            first(q)
        if 1 <= q < 9:
            second(q - 1)
        if 2 <= q:
            third(q - 2)
    for q in range(8):
        relay(q, sibling, sibling, 2).wait_recv()
        relay(q, flip(down), sibling, 4).wait_recv()
        relay(q, flip(up), sibling, 5).wait_recv()
        relay(q, flip(across), sibling, 6).wait_recv()
    for copy in started:
        copy.wait_send()
    for dz in ZORDER:
        for dx in range(4):
            if dz or dx:
                piece(dz, dx).wait_send()


def spread(grad):
    return pl.pallas_call(
        spread_kernel,
        out_shape=jax.ShapeDtypeStruct((N, N), bf16),
        in_specs=[pl.BlockSpec(memory_space=pl.ANY)],
        out_specs=pl.BlockSpec(memory_space=pl.ANY),
        scratch_shapes=[
            pltpu.SemaphoreType.DMA,
            pltpu.SemaphoreType.DMA((32,)),
            pltpu.SemaphoreType.DMA((32,)),
            pltpu.SemaphoreType.DMA((7, 8)),
            pltpu.SemaphoreType.DMA((7, 8)),
        ],
        compiler_params=pltpu.CompilerParams(collective_id=0, has_side_effects=True),
    )(grad)


def transpose_into(source, target):
    def step(k, _):
        i, j = k // 8, lax.rem(k, 8)
        target[at(j * TILE, TILE), at(i * TILE, TILE)] = source[
            at(i * TILE, TILE), at(j * TILE, TILE)
        ].T
        return 0

    lax.fori_loop(0, 64, step, 0)


def gram(operand, stat):
    def tile(i, distance):
        j = lax.rem(i + distance, 8)
        rows, columns = at(i * TILE, TILE), at(j * TILE, TILE)
        value = lax.dot_general(
            operand[rows, :], operand[columns, :], NT, preferred_element_type=f32
        ) * (1.0 / N)
        stat[rows, columns] = value
        if distance in (1, 2, 3):
            stat[columns, rows] = value.T

    def row(i, _):
        for distance in range(5):
            tile(i, distance)
        return 0

    lax.fori_loop(0, 8, row, 0)


def eye(size):
    return lax.broadcasted_iota(jnp.int32, (size, size), 0) == lax.broadcasted_iota(
        jnp.int32, (size, size), 1
    )


def add_diagonal(stat, value):
    def step(i, trace):
        where = (at(i * TILE, TILE), at(i * TILE, TILE))
        old, mask = stat[where], eye(TILE)
        stat[where] = jnp.where(mask, old + value, old)
        return trace + jnp.sum(jnp.where(mask, old, 0.0), keepdims=True)

    return lax.fori_loop(0, 8, step, jnp.zeros((1, 1), f32))


def fold(value):
    parts = value.reshape(value.shape[0] // 8, 8, LANES)
    total = parts[0]
    for q in range(1, parts.shape[0]):
        total = total + parts[q]
    return total


def power(stat, rows=128):
    count = N // LANES
    blocks = N // rows

    def images(i, vector):
        where = at(i * rows, rows)
        total = stat[where, 0:LANES] * vector[0][:1]
        for k in range(1, count):
            total = total + stat[where, k * LANES : (k + 1) * LANES] * vector[k][:1]
        return jnp.sum(total, axis=1, keepdims=True)

    def shares(i, image, sums):
        where = at(i * rows, rows)
        return tuple(
            sums[k] + fold(stat[where, k * LANES : (k + 1) * LANES] * image)
            for k in range(count)
        )

    def double(_, carry):
        vector, _norm = carry

        def body(i, state):
            image, sums, squares = state
            later = images(i + 1, vector)
            return later, shares(i, image, sums), squares + image * image

        image, sums, squares = lax.fori_loop(
            0,
            blocks - 1,
            body,
            (
                images(0, vector),
                tuple(jnp.zeros((8, LANES), f32) for _ in range(count)),
                jnp.zeros((rows, 1), f32),
            ),
        )
        sums = shares(blocks - 1, image, sums)
        first = jnp.sum(squares + image * image, axis=0, keepdims=True)
        result = [jnp.sum(s, axis=0, keepdims=True) for s in sums]
        square = result[0] * result[0]
        for k in range(1, count):
            square = square + result[k] * result[k]
        second = jnp.sum(square, axis=1, keepdims=True)
        norm = jnp.sqrt(second) / jnp.sqrt(first)
        inverse = 1.0 / jnp.sqrt(second)
        return tuple(jnp.broadcast_to(r * inverse, (8, LANES)) for r in result), norm

    start = tuple(jnp.full((8, LANES), 1.0 / math.sqrt(N), f32) for _ in range(count))
    return lax.fori_loop(0, PSTEPS // 2, double, (start, jnp.ones((1, 1), f32)))[1]


def build(stat, norm, near, rows=128):
    scale = -0.25 / norm
    count = N // LANES

    def body(i, sums):
        where = at(i * rows, rows)
        out = []
        for k in range(count):
            columns = slice(k * LANES, (k + 1) * LANES)
            value = (stat[where, columns] * scale).astype(bf16)
            near[where, columns] = value
            wide = value.astype(f32)
            out.append(sums[k] + fold(wide * wide))
        return tuple(out)

    sums = lax.fori_loop(
        0, N // rows, body, tuple(jnp.zeros((8, LANES), f32) for _ in range(count))
    )

    def shift(i, _):
        where = (at(i * TILE, TILE), at(i * TILE, TILE))
        value = near[where].astype(f32)
        near[where] = jnp.where(eye(TILE), value - 1.25, value).astype(bf16)
        return 0

    lax.fori_loop(0, 8, shift, 0)
    return [jnp.sum(s, axis=0, keepdims=True) for s in sums]


def times(left, right, finish, width=1024):
    def step(j, _):
        columns = at(j * width, width)
        finish(columns, jnp.dot(left[...], right[:, columns], preferred_element_type=f32))
        return 0

    lax.fori_loop(0, N // width, step, 0)


def rounding(value):
    return value.astype(bf16).astype(f32) - value


def refresh_kernel(
    block,
    update,
    whole,
    near,
    stat,
    wide,
    h0,
    h1,
    h2,
    mixed,
    square_diag,
    delta,
    diags,
    totals,
    load_sem,
    mixed_sem,
    diag_send,
    diag_recv,
    total_send,
    total_recv,
    out_sem,
):
    dp = lax.axis_index("dp")
    grp = lax.axis_index("grp")
    y, core = grp // 2, lax.rem(grp, 2)
    side = lax.rem(dp, 2)
    pair = dp + 1 - 2 * side
    sibling = grp + 1 - 2 * core
    starts = (HALF * (4 * y + side), HALF * (4 * y + side + 2))

    load = pltpu.make_async_copy(block, whole, load_sem)
    load.start()
    peers = []
    for k in range(1, 8):
        d, s = k // 4, k % 4
        peers.append(
            {"dp": pair if d else dp, "grp": lax.rem(y + s, 4) * 2 + core}
        )
    barrier = pltpu.get_barrier_semaphore()
    for peer in peers + [{"grp": sibling}]:
        pl.semaphore_signal(barrier, inc=1, device_id=peer, device_id_type=MESH)
    pl.semaphore_wait(barrier, 8)
    load.wait()

    @pl.when(core == 0)
    def _():
        gram(whole, stat)

    @pl.when(core == 1)
    def _():
        transpose_into(whole, near)
        gram(near, stat)

    trace = add_diagonal(stat, damping)
    norm = power(stat)
    add_diagonal(stat, -5.0 * norm)
    square = build(stat, norm, near)
    b0, b1 = stat.at[0:TILE], stat.at[TILE : 2 * TILE]
    for k in range(N // LANES):
        square_diag[0:1, k * LANES : (k + 1) * LANES] = rounding(square[k])
    delta[...] = jnp.zeros_like(delta)

    tiles = [(at(HALF * i, HALF), at(starts[i], HALF)) for i in range(2)]
    mask = eye(HALF)

    for rows, columns in tiles:
        h0[rows, :] = near[columns, :]
        value = near[columns, columns].astype(f32)
        h0[rows, columns] = jnp.where(mask, value + 1.25, value).astype(bf16)

    def finish_q(s, value):
        h1[:, s] = (value + 1.25 * h0[:, s].astype(f32)).astype(bf16)

    times(h0, near, finish_q)

    def finish_a(s, value):
        value = value + 1.25 * h1[:, s].astype(f32)
        b0[:, s] = value
        h0[:, s] = value.astype(bf16)

    times(h1, near, finish_a)
    middle = []
    for rows, columns in tiles:
        value = b0[rows, columns]
        middle.append(jnp.sum(jnp.where(mask, value, 0.0), axis=1, keepdims=True))
        h0[rows, columns] = jnp.where(mask, 0.0, value).astype(bf16)
    for i, (rows, columns) in enumerate(tiles):
        wide[rows, :] = jnp.broadcast_to(middle[i], (HALF, LANES))

    def finish_p4(s, value):
        for i, (rows, columns) in enumerate(tiles):
            part = (
                value[HALF * i : HALF * (i + 1)]
                + 1.25 * b0[rows, s]
                + wide[rows, 0:1] * near[columns, s].astype(f32)
                + h1[rows, s].astype(f32) * square_diag[0:1, s]
            )
            b1[rows, s] = part
            h2[rows, s] = part.astype(bf16)

    times(h0, near, finish_p4)

    def row_of(values):
        return jnp.sum(jnp.where(mask, values, 0.0), axis=0, keepdims=True)

    for i, (rows, columns) in enumerate(tiles):
        delta[i, 0:1, :] = row_of(rounding(b1[rows, columns]))

    def finish_t1(s, value):
        fifth = value + 1.25 * h2[:, s].astype(f32)
        value = fifth - 1.25 * b1[:, s]
        b0[:, s] = value
        h0[:, s] = value.astype(bf16)

    times(h2, near, finish_t1)
    for i, (rows, columns) in enumerate(tiles):
        value = b0[rows, columns]
        value = jnp.where(mask, value + 1.25, value)
        h0[rows, columns] = value.astype(bf16)
        delta[i, 1:2, :] = row_of(rounding(value))

    def finish_x(s, value):
        value = value + 1.25 * h0[:, s].astype(f32)
        b1[:, s] = value
        h1[:, s] = value.astype(bf16)

    times(h0, near, finish_x)
    for i, (rows, columns) in enumerate(tiles):
        delta[i, 2:3, :] = row_of(rounding(b1[rows, columns]))

    def mixed_copy():
        return pltpu.make_async_remote_copy(
            src_ref=h2,
            dst_ref=mixed,
            send_sem=mixed_sem.at[0],
            recv_sem=mixed_sem.at[1],
            device_id={"grp": sibling},
            device_id_type=MESH,
        )

    def result_copy():
        return pltpu.make_async_remote_copy(
            src_ref=h0.at[0:HALF],
            dst_ref=update.at[0],
            send_sem=out_sem.at[0],
            recv_sem=out_sem.at[1],
            device_id={"grp": sibling},
            device_id_type=MESH,
        )

    @pl.when(core == 0)
    def _():
        def finish_y(s, value):
            h2[:, s] = value.astype(bf16)

        times(h1, whole, finish_y)
        mixed_copy().start()
        mixed_copy().wait_send()
        result_copy().wait_recv()

    @pl.when(core == 1)
    def _():
        copies = []
        for k, peer in enumerate(peers):
            for i, (rows, columns) in enumerate(tiles):
                copies.append(
                    pltpu.make_async_remote_copy(
                        src_ref=delta.at[i],
                        dst_ref=diags.at[:, columns],
                        send_sem=diag_send.at[k, i],
                        recv_sem=diag_recv.at[k, i],
                        device_id=peer,
                        device_id_type=MESH,
                    )
                )
        for copy in copies:
            copy.start()
        for i, (rows, columns) in enumerate(tiles):
            diags[:, columns] = delta[i]
        for copy in copies:
            copy.wait()
        mixed_copy().wait_recv()

        def y_of(s):
            return mixed[:, s].astype(f32)

        def finish_1(s, value):
            value = value + 1.25 * y_of(s)
            b0[:, s] = value
            h0[:, s] = value.astype(bf16)

        times(mixed, near, finish_1)

        def finish_2(s, value):
            value = value + 1.25 * b0[:, s] + y_of(s) * square_diag[0:1, s]
            b1[:, s] = value
            h2[:, s] = value.astype(bf16)

        times(h0, near, finish_2)

        def finish_3(s, value):
            value = value + 1.25 * b1[:, s]
            b0[:, s] = value
            h0[:, s] = value.astype(bf16)

        times(h2, near, finish_3)

        def finish_4(s, value):
            value = value + 1.25 * b0[:, s] + b1[:, s] * square_diag[0:1, s]
            b0[:, s] = value
            h2[:, s] = (value + y_of(s) * diags[0:1, s]).astype(bf16)

        times(h0, near, finish_4)

        def finish_5(s, value):
            fourth, mix = b0[:, s], y_of(s)
            fifth = value + 1.25 * (fourth + mix * diags[0:1, s])
            value = 1.25 * (mix - fourth) + fifth + mix * diags[1:2, s]
            b1[:, s] = value
            h0[:, s] = value.astype(bf16)

        times(h2, near, finish_5)

        def finish_6(s, value):
            b0[:, s] = value + 1.25 * b1[:, s] + y_of(s) * diags[2:3, s]

        times(h0, near, finish_6)

        def squares(k, total):
            value = b0[:, at(k * LANES, LANES)]
            return total + fold(value * value)

        partial = lax.fori_loop(0, N // LANES, squares, jnp.zeros((8, LANES), f32))
        totals[0] = partial
        copies = []
        for k, peer in enumerate(peers):
            copies.append(
                pltpu.make_async_remote_copy(
                    src_ref=totals.at[0],
                    dst_ref=totals.at[k + 1],
                    send_sem=total_send.at[k],
                    recv_sem=total_recv.at[k],
                    device_id=peer,
                    device_id_type=MESH,
                )
            )
        for copy in copies:
            copy.start()
        for copy in copies:
            copy.wait()
        total = totals[0]
        for k in range(1, 8):
            total = total + totals[k]
        upd = jnp.sum(jnp.sum(total, axis=0, keepdims=True), axis=1, keepdims=True)
        factor = jnp.sqrt(trace / N) * lax.rsqrt(upd / (N * N) + graft_floor)

        def scaled(k, _):
            s = at(k * TILE, TILE)
            h0[:, s] = (b0[:, s] * factor).astype(bf16)
            return 0

        lax.fori_loop(0, N // TILE, scaled, 0)
        result_copy().start()
        keep = pltpu.make_async_copy(h0.at[HALF:TILE], update.at[0], load_sem)
        keep.start()
        keep.wait()
        result_copy().wait_send()


def refresh(block):
    return pl.pallas_call(
        refresh_kernel,
        out_shape=jax.ShapeDtypeStruct((1, HALF, N), bf16),
        in_specs=[pl.BlockSpec(memory_space=pl.ANY)],
        out_specs=pl.BlockSpec(memory_space=pl.ANY),
        scratch_shapes=[
            pltpu.VMEM((N, N), bf16),
            pltpu.VMEM((N, N), bf16),
            pltpu.VMEM((N, N), f32),
            pltpu.VMEM((TILE, LANES), f32),
            pltpu.VMEM((TILE, N), bf16),
            pltpu.VMEM((TILE, N), bf16),
            pltpu.VMEM((TILE, N), bf16),
            pltpu.VMEM((TILE, N), bf16),
            pltpu.VMEM((8, N), f32),
            pltpu.VMEM((2, 8, LANES), f32),
            pltpu.VMEM((8, N), f32),
            pltpu.VMEM((8, 8, LANES), f32),
            pltpu.SemaphoreType.DMA,
            pltpu.SemaphoreType.DMA((2,)),
            pltpu.SemaphoreType.DMA((7, 2)),
            pltpu.SemaphoreType.DMA((7, 2)),
            pltpu.SemaphoreType.DMA((7,)),
            pltpu.SemaphoreType.DMA((7,)),
            pltpu.SemaphoreType.DMA((2,)),
        ],
        compiler_params=pltpu.CompilerParams(
            collective_id=1, has_side_effects=True, vmem_limit_bytes=62 * 1024 * 1024
        ),
    )(block)


def per_device(grad):
    return refresh(spread(grad))


def solution(mesh):
    return jax.shard_map(
        per_device,
        mesh=mesh,
        in_specs=(P(None, "dp", None),),
        out_specs=P("dp", "grp", None),
        check_vma=False,
    )
```

time: 645 us -> 146 us (0.23)
  waiting for transfers between devices: 372 us -> 0 us
  blocking collectives: 149 us -> 0 us
  Pallas kernels: 0 us -> 144 us
  matrix products: 51.4 us -> 0 us
  between operations: 20.3 us -> 0.02 us
  other arithmetic: 18.7 us -> 0 us
  local copies, waits for them, and re-layouts: 19.1 us -> 1.88 us
  starting transfers between devices: 13.6 us -> 0 us
    all_to_all x1 -> x0, waiting for transfers between devices: 187 us -> none  [per_device(): lax.all_to_all(sent, 'dp', split_axis=0, concat_axis=1, tiled=True)[0]]
    all_gather x3 -> x0, waiting for transfers between devices: 161 us -> none  [the longest x1 57.7 us: per_device(): t_full = lax.all_gather(t_zero, 'grp', axis=0, tiled=True)]
    pallas_call x0 -> x2, Pallas kernels: none -> 144 us  [the longest x1 81.9 us: refresh(): pl.pallas_call(refresh_kernel, out_shape=jax.ShapeDtypeStruct((1, HALF, N...]
    psum x1 -> x0, blocking collectives: 75.9 us -> none  [per_device(): lax.psum((onehot * grad_sq, onehot * upd_sq), ('dp', 'grp'))]
    all_gather x8 -> x0, blocking collectives: 73.6 us -> none  [per_device(): image = lax.all_gather(piece, 'grp', axis=0, tiled=True)]
    dot_general x13 -> x0, matrix products: 51.4 us -> none  [the longest x8 13.8 us: per_device(): piece = jnp.dot(stat, vector, precision=lax.Precision.HIGHEST)]
    ppermute x1 -> x0, waiting for transfers between devices: 23.3 us -> none  [from_partner(): return lax.ppermute(value, axis, pairs)]
    squeeze x1 -> x0, local copies, waits for them, and re-layouts: 12.3 us -> none  [per_device(): lax.all_to_all(sent, 'dp', split_axis=0, concat_axis=1, tiled=True)[0]]
  transfers between devices with their start and end apart: 5 -> 0, of which waited for: 5 -> 0; matrix products, arithmetic and copies ran while one was open for 0% -> 0% of each run, Pallas kernels for 0% -> 0%
where the time goes in v1:
time: 146 us
  Pallas kernels  144 us (99%)
  local copies, waits for them, and re-layouts  1.88 us (1%)
    pallas_call x1, Pallas kernels, refresh(): pl.pallas_call(refresh_kernel, out_shape=jax.ShapeDtypeStruct((1, HALF, N...  81.9 us
    pallas_call x1, Pallas kernels, spread(): pl.pallas_call(spread_kernel, out_shape=jax.ShapeDtypeStruct((N, N), bf16...  61.7 us

profile of v1, /device:TPU:1, one launch (start us, length us, event | category | flops | bytes accessed | tf_op | source)
XLA Modules:
  0.0 145.5 jit_solution(11581916319920439982)
XLA Ops:
  0.0 61.7 %shard_map.17.block = bf16[2048,2048]{1,0:T(8,128)(2,1)} custom-call(bf16[16,64,2048]{2,1,0:T(8,128)(2,1)} %grad.1), custom_call_target="tpu_custom_call" | custom-call | tf_op jit(solution)/shard_map/pallas_call | solution.py:142
  61.7 81.9 %shard_map.18 = bf16[1,128,2048]{2,1,0:T(8,128)(2,1)} custom-call(bf16[2048,2048]{1,0:T(8,128)(2,1)} %shard_map.17.block), custom_call_target="tpu_custom_call" | custom-call | tf_op jit(solution)/shard_map/pallas_call | solution.py:576
  143.6 1.9 %copy.3 = bf16[1,128,2048]{2,1,0:T(8,128)(2,1)} copy(bf16[1,128,2048]{2,1,0:T(8,128)(2,1)} %shard_map.18) | data formatting | bytes 1048576

commit v2 on v1

--- a/solution.py
+++ b/solution.py
@@ -1,4 +1,3 @@
-import functools
 import math
 
 import jax
@@ -27,162 +26,63 @@
     return pl.ds(pl.multiple_of(start, unit or size), size)
 
 
-def spread_kernel(grad, block, local_sem, send1, recv1, send2, recv2):
-    dp = lax.axis_index("dp")
-    grp = lax.axis_index("grp")
-    z, x = dp // 4, lax.rem(dp, 4)
-    y, core = grp // 2, lax.rem(grp, 2)
-    up = lax.rem(y + 1, 4) * 2 + core
-    down = lax.rem(y + 3, 4) * 2 + core
-    across = lax.rem(y + 2, 4) * 2 + core
-    sibling = grp + 1 - 2 * core
-
-    def flip(g):
-        return g + 1 - 2 * core
-
-    barrier = pltpu.get_barrier_semaphore()
-
-    def greet(k, _):
-        pl.semaphore_signal(
-            barrier, inc=1, device_id={"dp": lax.rem(dp + k, 32)}, device_id_type=MESH
-        )
+def tile_of(block):
+    return slice(block * TILE, (block + 1) * TILE)
+
+
+def gram_rows(whole, stat, last):
+    new = tile_of(last)
+
+    def tile(i, _):
+        rows = at(i * TILE, TILE)
+        value = lax.dot_general(
+            whole[rows, :], whole[new, :], NT, preferred_element_type=f32
+        )
+        stat[rows, new] = value
+        stat[new, rows] = value.T
         return 0
 
-    lax.fori_loop(1, 32, greet, 0)
-    for g in (up, down, sibling):
-        pl.semaphore_signal(barrier, inc=1, device_id={"grp": g}, device_id_type=MESH)
-    pl.semaphore_wait(barrier, 34)
-
-    def piece(dz, dx):
-        target = lax.rem(z + dz, 8) * 4 + lax.rem(x + dx, 4)
-        return pltpu.make_async_remote_copy(
-            src_ref=grad.at[target // 2, :, at(grp * TILE, TILE)],
-            dst_ref=block.at[at(dp * 64, 64), at(grp * TILE, TILE)],
-            send_sem=send1.at[dz * 4 + dx],
-            recv_sem=recv1.at[dz * 4 + dx],
-            device_id={"dp": target},
-            device_id_type=MESH,
-        )
-
-    own = pltpu.make_async_copy(
-        grad.at[dp // 2, :, at(grp * TILE, TILE)],
-        block.at[at(dp * 64, 64), at(grp * TILE, TILE)],
-        local_sem,
-    )
-    own.start()
-    for dz in ZORDER:
-        for dx in range(4):
-            if dz or dx:
-                piece(dz, dx).start()
-
-    def relay(q, column, target, slot):
-        rows = at(lax.rem(z + 8 - ZORDER[q], 8) * TILE, TILE)
-        ref = block.at[rows, at(column * TILE, TILE)]
-        return pltpu.make_async_remote_copy(
-            src_ref=ref,
-            dst_ref=ref,
-            send_sem=send2.at[slot, q],
-            recv_sem=recv2.at[slot, q],
-            device_id={"grp": target},
-            device_id_type=MESH,
-        )
-
-    started = []
-
-    def go(*args):
-        copy = relay(*args)
-        copy.start()
-        started.append(copy)
-
-    def first(q):
-        for dx in range(4):
-            if ZORDER[q] or dx:
-                piece(ZORDER[q], dx).wait_recv()
-            else:
-                own.wait()
-        go(q, grp, up, 0)
-        go(q, grp, down, 1)
-        go(q, grp, sibling, 2)
-
-    def second(q):
-        relay(q, down, up, 0).wait_recv()
-        if q % 2 == 0:
-            go(q, down, up, 3)
-        relay(q, up, down, 1).wait_recv()
-        if q % 2:
-            go(q, up, down, 3)
-        go(q, down, sibling, 4)
-        go(q, up, sibling, 5)
-
-    def third(q):
-        relay(q, across, up, 3).wait_recv()
-        go(q, across, sibling, 6)
-
-    for q in range(8 + 2):
-        if q < 8:
-            first(q)
-        if 1 <= q < 9:
-            second(q - 1)
-        if 2 <= q:
-            third(q - 2)
-    for q in range(8):
-        relay(q, sibling, sibling, 2).wait_recv()
-        relay(q, flip(down), sibling, 4).wait_recv()
-        relay(q, flip(up), sibling, 5).wait_recv()
-        relay(q, flip(across), sibling, 6).wait_recv()
-    for copy in started:
-        copy.wait_send()
-    for dz in ZORDER:
-        for dx in range(4):
-            if dz or dx:
-                piece(dz, dx).wait_send()
-
-
-def spread(grad):
-    return pl.pallas_call(
-        spread_kernel,
-        out_shape=jax.ShapeDtypeStruct((N, N), bf16),
-        in_specs=[pl.BlockSpec(memory_space=pl.ANY)],
-        out_specs=pl.BlockSpec(memory_space=pl.ANY),
-        scratch_shapes=[
-            pltpu.SemaphoreType.DMA,
-            pltpu.SemaphoreType.DMA((32,)),
-            pltpu.SemaphoreType.DMA((32,)),
-            pltpu.SemaphoreType.DMA((7, 8)),
-            pltpu.SemaphoreType.DMA((7, 8)),
-        ],
-        compiler_params=pltpu.CompilerParams(collective_id=0, has_side_effects=True),
-    )(grad)
-
-
-def transpose_into(source, target):
-    def step(k, _):
-        i, j = k // 8, lax.rem(k, 8)
-        target[at(j * TILE, TILE), at(i * TILE, TILE)] = source[
-            at(i * TILE, TILE), at(j * TILE, TILE)
-        ].T
-        return 0
-
-    lax.fori_loop(0, 64, step, 0)
-
-
-def gram(operand, stat):
+    lax.fori_loop(0, last + 1, tile, 0)
+
+
+def gram_depth(turned, stat, step):
+    depth = slice(step * 512, (step + 1) * 512)
+
     def tile(i, distance):
         j = lax.rem(i + distance, 8)
         rows, columns = at(i * TILE, TILE), at(j * TILE, TILE)
         value = lax.dot_general(
-            operand[rows, :], operand[columns, :], NT, preferred_element_type=f32
-        ) * (1.0 / N)
+            turned[rows, depth], turned[columns, depth], NT, preferred_element_type=f32
+        )
+        if step:
+            value = value + stat[rows, columns]
         stat[rows, columns] = value
-        if distance in (1, 2, 3):
+        if distance and step == 3:
             stat[columns, rows] = value.T
 
     def row(i, _):
-        for distance in range(5):
+        for distance in range(4):
             tile(i, distance)
         return 0
 
     lax.fori_loop(0, 8, row, 0)
+
+    def opposite(i, _):
+        tile(i, 4)
+        return 0
+
+    lax.fori_loop(0, 4, opposite, 0)
+
+
+def turn(whole, turned, group):
+    rows = tile_of(group)
+
+    def step(j, _):
+        columns = at(j * TILE, TILE)
+        turned[columns, rows] = whole[rows, columns].T
+        return 0
+
+    lax.fori_loop(0, 8, step, 0)
 
 
 def eye(size):
@@ -215,10 +115,13 @@
 
     def images(i, vector):
         where = at(i * rows, rows)
-        total = stat[where, 0:LANES] * vector[0][:1]
-        for k in range(1, count):
-            total = total + stat[where, k * LANES : (k + 1) * LANES] * vector[k][:1]
-        return jnp.sum(total, axis=1, keepdims=True)
+        total = None
+        for k in range(count):
+            part = stat[where, k * LANES : (k + 1) * LANES].reshape(rows // 8, 8, LANES)
+            part = part * vector[k][None]
+            total = part if total is None else total + part
+        total = jnp.sum(total.reshape(rows, LANES), axis=1, keepdims=True)
+        return jnp.broadcast_to(total, (rows, LANES))
 
     def shares(i, image, sums):
         where = at(i * rows, rows)
@@ -242,11 +145,11 @@
             (
                 images(0, vector),
                 tuple(jnp.zeros((8, LANES), f32) for _ in range(count)),
-                jnp.zeros((rows, 1), f32),
+                jnp.zeros((rows, LANES), f32),
             ),
         )
         sums = shares(blocks - 1, image, sums)
-        first = jnp.sum(squares + image * image, axis=0, keepdims=True)
+        first = jnp.sum(squares + image * image, axis=0, keepdims=True)[:, 0:1]
         result = [jnp.sum(s, axis=0, keepdims=True) for s in sums]
         square = result[0] * result[0]
         for k in range(1, count):
@@ -269,24 +172,23 @@
         out = []
         for k in range(count):
             columns = slice(k * LANES, (k + 1) * LANES)
-            value = (stat[where, columns] * scale).astype(bf16)
-            near[where, columns] = value
-            wide = value.astype(f32)
-            out.append(sums[k] + fold(wide * wide))
+            value = stat[where, columns] * scale
+            near[where, columns] = value.astype(bf16)
+            out.append(sums[k] + fold(value * value))
         return tuple(out)
 
     sums = lax.fori_loop(
         0, N // rows, body, tuple(jnp.zeros((8, LANES), f32) for _ in range(count))
     )
-
-    def shift(i, _):
-        where = (at(i * TILE, TILE), at(i * TILE, TILE))
-        value = near[where].astype(f32)
-        near[where] = jnp.where(eye(TILE), value - 1.25, value).astype(bf16)
-        return 0
-
-    lax.fori_loop(0, 8, shift, 0)
-    return [jnp.sum(s, axis=0, keepdims=True) for s in sums]
+    diagonal = []
+    for k in range(count):
+        where = (slice(k * LANES, (k + 1) * LANES),) * 2
+        plain = stat[where] * scale
+        entry = (plain + 1.25).astype(bf16).astype(f32)
+        near[where] = jnp.where(eye(LANES), entry - 1.25, plain).astype(bf16)
+        extra = jnp.where(eye(LANES), entry * entry - plain * plain, 0.0)
+        diagonal.append(jnp.sum(sums[k] + fold(extra), axis=0, keepdims=True))
+    return diagonal
 
 
 def times(left, right, finish, width=1024):
@@ -303,11 +205,12 @@
 
 
 def refresh_kernel(
-    block,
+    grad,
     update,
     whole,
     near,
     stat,
+    staging,
     wide,
     h0,
     h1,
@@ -317,7 +220,15 @@
     delta,
     diags,
     totals,
-    load_sem,
+    local_sem,
+    z_send,
+    z_recv,
+    x_send,
+    x_recv,
+    y_send,
+    y_recv,
+    s_send,
+    s_recv,
     mixed_sem,
     diag_send,
     diag_recv,
@@ -327,38 +238,154 @@
 ):
     dp = lax.axis_index("dp")
     grp = lax.axis_index("grp")
+    z, x = dp // 4, lax.rem(dp, 4)
     y, core = grp // 2, lax.rem(grp, 2)
-    side = lax.rem(dp, 2)
+    side, half = lax.rem(x, 2), x // 2
     pair = dp + 1 - 2 * side
     sibling = grp + 1 - 2 * core
-    starts = (HALF * (4 * y + side), HALF * (4 * y + side + 2))
-
-    load = pltpu.make_async_copy(block, whole, load_sem)
-    load.start()
+    up = lax.rem(y + 1, 4) * 2 + core
+    down = lax.rem(y + 3, 4) * 2 + core
+    parity = lax.rem(y, 2)
+    chunk = parity * 2 + core
+    other_chunk = (1 - parity) * 2 + core
+
     peers = []
     for k in range(1, 8):
         d, s = k // 4, k % 4
-        peers.append(
-            {"dp": pair if d else dp, "grp": lax.rem(y + s, 4) * 2 + core}
-        )
+        peers.append({"dp": pair if d else dp, "grp": lax.rem(y + s, 4) * 2 + core})
+    crossing = [
+        {"dp": z * 4 + 2 * (1 - half) + side},
+        {"dp": z * 4 + 2 * (1 - half) + 1 - side},
+    ]
+    along = [{"dp": lax.rem(z + dz, 8) * 4 + x} for dz in ZORDER]
+    greeted = along[1:] + crossing + peers + [{"grp": sibling}]
     barrier = pltpu.get_barrier_semaphore()
-    for peer in peers + [{"grp": sibling}]:
-        pl.semaphore_signal(barrier, inc=1, device_id=peer, device_id_type=MESH)
-    pl.semaphore_wait(barrier, 8)
-    load.wait()
-
-    @pl.when(core == 0)
-    def _():
-        gram(whole, stat)
-
-    @pl.when(core == 1)
-    def _():
-        transpose_into(whole, near)
-        gram(near, stat)
-
-    trace = add_diagonal(stat, damping)
+    for device in greeted:
+        pl.semaphore_signal(barrier, inc=1, device_id=device, device_id_type=MESH)
+    pl.semaphore_wait(barrier, len(greeted))
+
+    def remote(src, dst, send, recv, device):
+        return pltpu.make_async_remote_copy(
+            src_ref=src,
+            dst_ref=dst,
+            send_sem=send,
+            recv_sem=recv,
+            device_id=device,
+            device_id_type=MESH,
+        )
+
+    own_columns = at(chunk * 512, 512)
+
+    def piece(q):
+        return whole.at[at(q * TILE + x * 64, 64), own_columns]
+
+    def block_of(q, same):
+        first = 2 * lax.rem(z + ZORDER[q], 8)
+        return grad.at[first + (half if same else 1 - half), :, own_columns]
+
+    def z_copies(q):
+        if q == 0:
+            return [
+                pltpu.make_async_copy(block_of(0, True), piece(0), local_sem.at[0]),
+                pltpu.make_async_copy(block_of(0, False), staging.at[0], local_sem.at[1]),
+            ]
+        return [
+            remote(block_of(q, True), piece(q), z_send.at[0, q], z_recv.at[0, q], along[q]),
+            remote(
+                block_of(q, False), staging.at[q], z_send.at[1, q], z_recv.at[1, q], along[q]
+            ),
+        ]
+
+    def x_copies(q):
+        copies = [remote(piece(q), piece(q), x_send.at[0, q], x_recv.at[0, q], {"dp": pair})]
+        for i, device in enumerate(crossing):
+            copies.append(
+                remote(
+                    staging.at[q], piece(q), x_send.at[i + 1, q], x_recv.at[i + 1, q], device
+                )
+            )
+        return copies
+
+    def part(q, which, i):
+        return whole.at[tile_of(q), at(which * 512 + i * TILE, TILE)]
+
+    def y_copies(q):
+        return [
+            remote(
+                part(q, chunk, i),
+                part(q, chunk, i),
+                y_send.at[i, q],
+                y_recv.at[i, q],
+                {"grp": device},
+            )
+            for i, device in enumerate((up, down))
+        ]
+
+    def s_copy(q, i):
+        ref = part(q, other_chunk, i - 1) if i else whole.at[tile_of(q), own_columns]
+        return remote(ref, ref, s_send.at[i, q], s_recv.at[i, q], {"grp": sibling})
+
+    for q in range(8):
+        for copy in z_copies(q):
+            copy.start()
+
+    def spread_x(q):
+        for copy in z_copies(q):
+            if q:
+                copy.wait_recv()
+            else:
+                copy.wait()
+        for copy in x_copies(q):
+            copy.start()
+
+    def spread_y(q):
+        for copy in x_copies(q):
+            copy.wait_recv()
+        for copy in y_copies(q):
+            copy.start()
+        s_copy(q, 0).start()
+
+    def spread_s(q):
+        for i, copy in enumerate(y_copies(q)):
+            copy.wait_recv()
+            s_copy(q, i + 1).start()
+
+    def use(q):
+        for i in range(3):
+            s_copy(q, i).wait_recv()
+
+        @pl.when(core == 0)
+        def _():
+            gram_rows(whole, stat, q)
+
+        @pl.when(core == 1)
+        def _():
+            turn(whole, near, q)
+            if q % 2:
+                gram_depth(near, stat, q // 2)
+
+    for step in range(8 + 3):
+        for lag, stage in enumerate((spread_x, spread_y, spread_s, use)):
+            if 0 <= step - lag < 8:
+                stage(step - lag)
+
+    for q in range(8):
+        for copy in (z_copies(q) if q else []) + x_copies(q) + y_copies(q):
+            copy.wait_send()
+        for i in range(3):
+            s_copy(q, i).wait_send()
+
+    def position(group):
+        distance = lax.rem(z + 8 - group // 2, 8)
+        place = jnp.where(
+            distance == 0, 0, jnp.where(distance <= 4, 2 * distance - 1, 16 - 2 * distance)
+        )
+        return HALF * jnp.where(core == 0, 2 * place + lax.rem(group, 2), group)
+
+    starts = (position(4 * y + side), position(4 * y + side + 2))
+
+    trace = add_diagonal(stat, N * damping)
     norm = power(stat)
-    add_diagonal(stat, -5.0 * norm)
     square = build(stat, norm, near)
     b0, b1 = stat.at[0:TILE], stat.at[TILE : 2 * TILE]
     for k in range(N // LANES):
@@ -557,7 +584,7 @@
         for k in range(1, 8):
             total = total + totals[k]
         upd = jnp.sum(jnp.sum(total, axis=0, keepdims=True), axis=1, keepdims=True)
-        factor = jnp.sqrt(trace / N) * lax.rsqrt(upd / (N * N) + graft_floor)
+        factor = jnp.sqrt(trace / (N * N)) * lax.rsqrt(upd / (N * N) + graft_floor)
 
         def scaled(k, _):
             s = at(k * TILE, TILE)
@@ -566,13 +593,14 @@
 
         lax.fori_loop(0, N // TILE, scaled, 0)
         result_copy().start()
-        keep = pltpu.make_async_copy(h0.at[HALF:TILE], update.at[0], load_sem)
+        keep = pltpu.make_async_copy(h0.at[HALF:TILE], update.at[0], local_sem.at[0])
         keep.start()
         keep.wait()
         result_copy().wait_send()
 
 
-def refresh(block):
+def refresh(grad):
+    dma = pltpu.SemaphoreType.DMA
     return pl.pallas_call(
         refresh_kernel,
         out_shape=jax.ShapeDtypeStruct((1, HALF, N), bf16),
@@ -582,6 +610,7 @@
             pltpu.VMEM((N, N), bf16),
             pltpu.VMEM((N, N), bf16),
             pltpu.VMEM((N, N), f32),
+            pltpu.VMEM((8, 64, 512), bf16),
             pltpu.VMEM((TILE, LANES), f32),
             pltpu.VMEM((TILE, N), bf16),
             pltpu.VMEM((TILE, N), bf16),
@@ -591,27 +620,31 @@
             pltpu.VMEM((2, 8, LANES), f32),
             pltpu.VMEM((8, N), f32),
             pltpu.VMEM((8, 8, LANES), f32),
-            pltpu.SemaphoreType.DMA,
-            pltpu.SemaphoreType.DMA((2,)),
-            pltpu.SemaphoreType.DMA((7, 2)),
-            pltpu.SemaphoreType.DMA((7, 2)),
-            pltpu.SemaphoreType.DMA((7,)),
-            pltpu.SemaphoreType.DMA((7,)),
-            pltpu.SemaphoreType.DMA((2,)),
+            dma((2,)),
+            dma((2, 8)),
+            dma((2, 8)),
+            dma((3, 8)),
+            dma((3, 8)),
+            dma((2, 8)),
+            dma((2, 8)),
+            dma((3, 8)),
+            dma((3, 8)),
+            dma((2,)),
+            dma((7, 2)),
+            dma((7, 2)),
+            dma((7,)),
+            dma((7,)),
+            dma((2,)),
         ],
         compiler_params=pltpu.CompilerParams(
-            collective_id=1, has_side_effects=True, vmem_limit_bytes=62 * 1024 * 1024
+            collective_id=0, has_side_effects=True, vmem_limit_bytes=62 * 1024 * 1024
         ),
-    )(block)
-
-
-def per_device(grad):
-    return refresh(spread(grad))
+    )(grad)
 
 
 def solution(mesh):
     return jax.shard_map(
-        per_device,
+        refresh,
         mesh=mesh,
         in_specs=(P(None, "dp", None),),
         out_specs=P("dp", "grp", None),

time: 146 us -> 126 us (0.86)
  Pallas kernels: 144 us -> 124 us
    pallas_call x1 -> x0, Pallas kernels: 61.7 us -> none  [spread(): pl.pallas_call(spread_kernel, out_shape=jax.ShapeDtypeStruct((N, N), bf16...]
    pallas_call x1, Pallas kernels: 81.9 us -> 124 us  [refresh(): pl.pallas_call(refresh_kernel, out_shape=jax.ShapeDtypeStruct((1, HALF, N...]
where the time goes in v2:
time: 126 us
  Pallas kernels  124 us (98%)
  local copies, waits for them, and re-layouts  1.88 us (1%)
    pallas_call x1, Pallas kernels, refresh(): pl.pallas_call(refresh_kernel, out_shape=jax.ShapeDtypeStruct((1, HALF, N...  124 us

profile of v2, /device:TPU:1, one launch (start us, length us, event | category | flops | bytes accessed | tf_op | source)
XLA Modules:
  0.0 126.0 jit_solution(10530558004023438377)
XLA Ops:
  0.0 124.1 %shard_map.17 = bf16[1,128,2048]{2,1,0:T(8,128)(2,1)} custom-call(bf16[16,64,2048]{2,1,0:T(8,128)(2,1)} %grad.1), custom_call_target="tpu_custom_call" | custom-call | tf_op jit(solution)/shard_map/pallas_call | solution.py:604
  124.1 1.9 %copy.3 = bf16[1,128,2048]{2,1,0:T(8,128)(2,1)} copy(bf16[1,128,2048]{2,1,0:T(8,128)(2,1)} %shard_map.17) | data formatting | bytes 1048576

commit v3 on v2

--- a/solution.py
+++ b/solution.py
@@ -20,6 +20,13 @@
 LANES = 128
 NT = (((1,), (1,)), ((), ()))
 ZORDER = (0, 1, 7, 2, 6, 3, 5, 4)
+DEPTHS = ((0, 1), (2, 3), (4, 5), (6, 7))
+MIRRORED = 7
+SPLIT = 1
+UNITS = 8 * SPLIT
+UNIT = TILE // SPLIT
+SHARE = UNIT // 4
+LAGS = (0, 2, 4, 6)
 
 
 def at(start, size, unit=None):
@@ -33,45 +40,50 @@
 def gram_rows(whole, stat, last):
     new = tile_of(last)
 
-    def tile(i, _):
-        rows = at(i * TILE, TILE)
+    def tile(rows):
         value = lax.dot_general(
             whole[rows, :], whole[new, :], NT, preferred_element_type=f32
         )
         stat[rows, new] = value
         stat[new, rows] = value.T
+
+    def double(i, _):
+        tile(at(i * 512, 512))
         return 0
 
-    lax.fori_loop(0, last + 1, tile, 0)
-
-
-def gram_depth(turned, stat, step):
-    depth = slice(step * 512, (step + 1) * 512)
+    lax.fori_loop(0, (last + 1) // 2, double, 0)
+    if last % 2 == 0:
+        tile(new)
+
+
+def gram_depth(turned, stat, groups):
+    depth = slice(groups[0] * TILE, (groups[-1] + 1) * TILE)
 
     def tile(i, distance):
-        j = lax.rem(i + distance, 8)
-        rows, columns = at(i * TILE, TILE), at(j * TILE, TILE)
+        j = lax.rem(i + distance, 4)
+        rows, columns = at(i * 512, 512), at(j * 512, 512)
         value = lax.dot_general(
             turned[rows, depth], turned[columns, depth], NT, preferred_element_type=f32
         )
-        if step:
+        if groups[0]:
             value = value + stat[rows, columns]
         stat[rows, columns] = value
-        if distance and step == 3:
+        if distance and groups[-1] == MIRRORED:
             stat[columns, rows] = value.T
 
     def row(i, _):
-        for distance in range(4):
+        for distance in range(4 if groups[-1] > MIRRORED else 2):
             tile(i, distance)
         return 0
 
-    lax.fori_loop(0, 8, row, 0)
-
-    def opposite(i, _):
-        tile(i, 4)
-        return 0
-
-    lax.fori_loop(0, 4, opposite, 0)
+    lax.fori_loop(0, 4, row, 0)
+
+    if groups[-1] <= MIRRORED:
+        def opposite(i, _):
+            tile(i, 2)
+            return 0
+
+        lax.fori_loop(0, 2, opposite, 0)
 
 
 def turn(whole, turned, group):
@@ -209,16 +221,20 @@
     update,
     whole,
     near,
+    other,
     stat,
     staging,
     wide,
+    rows_near,
     h0,
     h1,
     h2,
     mixed,
     square_diag,
+    square_right,
     delta,
     diags,
+    result,
     totals,
     local_sem,
     z_send,
@@ -229,12 +245,12 @@
     y_recv,
     s_send,
     s_recv,
+    factor_sem,
     mixed_sem,
     diag_send,
     diag_recv,
     total_send,
     total_recv,
-    out_sem,
 ):
     dp = lax.axis_index("dp")
     grp = lax.axis_index("grp")
@@ -277,23 +293,23 @@
     own_columns = at(chunk * 512, 512)
 
     def piece(q):
-        return whole.at[at(q * TILE + x * 64, 64), own_columns]
+        return whole.at[at(q * UNIT + x * SHARE, SHARE), own_columns]
 
     def block_of(q, same):
-        first = 2 * lax.rem(z + ZORDER[q], 8)
-        return grad.at[first + (half if same else 1 - half), :, own_columns]
+        first = 2 * lax.rem(z + ZORDER[q // SPLIT], 8)
+        rows = pl.ds(q % SPLIT * SHARE, SHARE)
+        return grad.at[first + (half if same else 1 - half), rows, own_columns]
 
     def z_copies(q):
-        if q == 0:
+        if q < SPLIT:
             return [
-                pltpu.make_async_copy(block_of(0, True), piece(0), local_sem.at[0]),
-                pltpu.make_async_copy(block_of(0, False), staging.at[0], local_sem.at[1]),
+                pltpu.make_async_copy(block_of(q, True), piece(q), local_sem.at[0, q]),
+                pltpu.make_async_copy(block_of(q, False), staging.at[q], local_sem.at[1, q]),
             ]
+        device = along[q // SPLIT]
         return [
-            remote(block_of(q, True), piece(q), z_send.at[0, q], z_recv.at[0, q], along[q]),
-            remote(
-                block_of(q, False), staging.at[q], z_send.at[1, q], z_recv.at[1, q], along[q]
-            ),
+            remote(block_of(q, True), piece(q), z_send.at[0, q], z_recv.at[0, q], device),
+            remote(block_of(q, False), staging.at[q], z_send.at[1, q], z_recv.at[1, q], device),
         ]
 
     def x_copies(q):
@@ -307,7 +323,7 @@
         return copies
 
     def part(q, which, i):
-        return whole.at[tile_of(q), at(which * 512 + i * TILE, TILE)]
+        return whole.at[pl.ds(q * UNIT, UNIT), at(which * 512 + i * TILE, TILE)]
 
     def y_copies(q):
         return [
@@ -322,16 +338,17 @@
         ]
 
     def s_copy(q, i):
-        ref = part(q, other_chunk, i - 1) if i else whole.at[tile_of(q), own_columns]
+        own = whole.at[pl.ds(q * UNIT, UNIT), own_columns]
+        ref = part(q, other_chunk, i - 1) if i else own
         return remote(ref, ref, s_send.at[i, q], s_recv.at[i, q], {"grp": sibling})
 
-    for q in range(8):
+    for q in range(UNITS):
         for copy in z_copies(q):
             copy.start()
 
     def spread_x(q):
         for copy in z_copies(q):
-            if q:
+            if q >= SPLIT:
                 copy.wait_recv()
             else:
                 copy.wait()
@@ -354,35 +371,44 @@
         for i in range(3):
             s_copy(q, i).wait_recv()
 
+        group = q // SPLIT
+        if (q + 1) % SPLIT:
+            return
+
         @pl.when(core == 0)
         def _():
-            gram_rows(whole, stat, q)
+            gram_rows(whole, stat, group)
 
         @pl.when(core == 1)
         def _():
-            turn(whole, near, q)
-            if q % 2:
-                gram_depth(near, stat, q // 2)
-
-    for step in range(8 + 3):
-        for lag, stage in enumerate((spread_x, spread_y, spread_s, use)):
-            if 0 <= step - lag < 8:
+            turn(whole, near, group)
+            for groups in DEPTHS:
+                if group == groups[-1]:
+                    gram_depth(near, stat, groups)
+
+    for step in range(UNITS + LAGS[-1]):
+        for lag, stage in zip(LAGS, (spread_x, spread_y, spread_s, use)):
+            if 0 <= step - lag < UNITS:
                 stage(step - lag)
 
-    for q in range(8):
-        for copy in (z_copies(q) if q else []) + x_copies(q) + y_copies(q):
+    for q in range(UNITS):
+        for copy in (z_copies(q) if q >= SPLIT else []) + x_copies(q) + y_copies(q):
             copy.wait_send()
         for i in range(3):
             s_copy(q, i).wait_send()
 
-    def position(group):
+    def region(group):
         distance = lax.rem(z + 8 - group // 2, 8)
         place = jnp.where(
             distance == 0, 0, jnp.where(distance <= 4, 2 * distance - 1, 16 - 2 * distance)
         )
-        return HALF * jnp.where(core == 0, 2 * place + lax.rem(group, 2), group)
-
-    starts = (position(4 * y + side), position(4 * y + side + 2))
+        return TILE * jnp.where(core == 0, place, group // 2)
+
+    def offset(i):
+        arrival = (i % 64) // SHARE * UNIT + (2 * side + i // 64) * SHARE + i % SHARE
+        return jnp.where(core == 0, arrival, side * HALF + i)
+
+    regions = (region(4 * y + side), region(4 * y + side + 2))
 
     trace = add_diagonal(stat, N * damping)
     norm = power(stat)
@@ -392,12 +418,40 @@
         square_diag[0:1, k * LANES : (k + 1) * LANES] = rounding(square[k])
     delta[...] = jnp.zeros_like(delta)
 
-    tiles = [(at(HALF * i, HALF), at(starts[i], HALF)) for i in range(2)]
-    mask = eye(HALF)
-
-    for rows, columns in tiles:
-        h0[rows, :] = near[columns, :]
-        value = near[columns, columns].astype(f32)
+    tiles = [(at(HALF * i, HALF), at(regions[i], TILE)) for i in range(2)]
+    entry = lax.broadcasted_iota(jnp.int32, (HALF, TILE), 0)
+    mask = lax.broadcasted_iota(jnp.int32, (HALF, TILE), 1) == offset(entry)
+
+    def factor_copies():
+        return [
+            remote(near, other, factor_sem.at[0], factor_sem.at[1], {"grp": sibling}),
+            remote(
+                square_diag, square_right, factor_sem.at[2], factor_sem.at[3], {"grp": sibling}
+            ),
+        ]
+
+    def factor_keeps():
+        return [
+            pltpu.make_async_copy(near, other, factor_sem.at[4]),
+            pltpu.make_async_copy(square_diag, square_right, factor_sem.at[5]),
+        ]
+
+    @pl.when(core == 1)
+    def _():
+        for copy in factor_copies() + factor_keeps():
+            copy.start()
+
+    for i, (rows, columns) in enumerate(tiles):
+        for j in range(4):
+            start = regions[i] + jnp.where(
+                core == 0,
+                (j % 2 * 32) // SHARE * UNIT + (2 * side + j // 2) * SHARE + (j % 2 * 32) % SHARE,
+                side * HALF + j * 32,
+            )
+            into = slice(i * HALF + j * 32, i * HALF + (j + 1) * 32)
+            rows_near[into, :] = near[at(start, 32), :]
+        h0[rows, :] = rows_near[rows, :]
+        value = rows_near[rows, columns].astype(f32)
         h0[rows, columns] = jnp.where(mask, value + 1.25, value).astype(bf16)
 
     def finish_q(s, value):
@@ -424,7 +478,7 @@
             part = (
                 value[HALF * i : HALF * (i + 1)]
                 + 1.25 * b0[rows, s]
-                + wide[rows, 0:1] * near[columns, s].astype(f32)
+                + wide[rows, 0:1] * rows_near[rows, s].astype(f32)
                 + h1[rows, s].astype(f32) * square_diag[0:1, s]
             )
             b1[rows, s] = part
@@ -433,7 +487,8 @@
     times(h0, near, finish_p4)
 
     def row_of(values):
-        return jnp.sum(jnp.where(mask, values, 0.0), axis=0, keepdims=True)
+        row = jnp.sum(jnp.where(mask, values, 0.0), axis=0, keepdims=True)
+        return jnp.where(side == 0, row[:, :HALF], row[:, HALF:])
 
     for i, (rows, columns) in enumerate(tiles):
         delta[i, 0:1, :] = row_of(rounding(b1[rows, columns]))
@@ -460,143 +515,135 @@
     for i, (rows, columns) in enumerate(tiles):
         delta[i, 2:3, :] = row_of(rounding(b1[rows, columns]))
 
-    def mixed_copy():
-        return pltpu.make_async_remote_copy(
-            src_ref=h2,
-            dst_ref=mixed,
-            send_sem=mixed_sem.at[0],
-            recv_sem=mixed_sem.at[1],
-            device_id={"grp": sibling},
-            device_id_type=MESH,
-        )
-
-    def result_copy():
-        return pltpu.make_async_remote_copy(
-            src_ref=h0.at[0:HALF],
-            dst_ref=update.at[0],
-            send_sem=out_sem.at[0],
-            recv_sem=out_sem.at[1],
-            device_id={"grp": sibling},
-            device_id_type=MESH,
-        )
+    mixed_copy = remote(
+        h2.at[HALF:TILE], mixed, mixed_sem.at[0], mixed_sem.at[1], {"grp": sibling}
+    )
+    diags_copy = remote(diags, diags, mixed_sem.at[2], mixed_sem.at[3], {"grp": sibling})
 
     @pl.when(core == 0)
     def _():
         def finish_y(s, value):
-            h2[:, s] = value.astype(bf16)
+            mixed[:, s] = value[:HALF].astype(bf16)
+            h2[HALF:TILE, s] = value[HALF:].astype(bf16)
 
         times(h1, whole, finish_y)
-        mixed_copy().start()
-        mixed_copy().wait_send()
-        result_copy().wait_recv()
+        mixed_copy.start()
+        for copy in factor_copies():
+            copy.wait_recv()
 
     @pl.when(core == 1)
     def _():
+        own = [at(HALF * (4 * y + side + 2 * i), HALF) for i in range(2)]
         copies = []
         for k, peer in enumerate(peers):
-            for i, (rows, columns) in enumerate(tiles):
+            for i, columns in enumerate(own):
                 copies.append(
-                    pltpu.make_async_remote_copy(
-                        src_ref=delta.at[i],
-                        dst_ref=diags.at[:, columns],
-                        send_sem=diag_send.at[k, i],
-                        recv_sem=diag_recv.at[k, i],
-                        device_id=peer,
-                        device_id_type=MESH,
+                    remote(
+                        delta.at[i],
+                        diags.at[:, columns],
+                        diag_send.at[k, i],
+                        diag_recv.at[k, i],
+                        peer,
                     )
                 )
         for copy in copies:
             copy.start()
-        for i, (rows, columns) in enumerate(tiles):
+        for i, columns in enumerate(own):
             diags[:, columns] = delta[i]
         for copy in copies:
             copy.wait()
-        mixed_copy().wait_recv()
-
-        def y_of(s):
-            return mixed[:, s].astype(f32)
-
-        def finish_1(s, value):
-            value = value + 1.25 * y_of(s)
-            b0[:, s] = value
-            h0[:, s] = value.astype(bf16)
-
-        times(mixed, near, finish_1)
-
-        def finish_2(s, value):
-            value = value + 1.25 * b0[:, s] + y_of(s) * square_diag[0:1, s]
-            b1[:, s] = value
-            h2[:, s] = value.astype(bf16)
-
-        times(h0, near, finish_2)
-
-        def finish_3(s, value):
-            value = value + 1.25 * b1[:, s]
-            b0[:, s] = value
-            h0[:, s] = value.astype(bf16)
-
-        times(h2, near, finish_3)
-
-        def finish_4(s, value):
-            value = value + 1.25 * b0[:, s] + b1[:, s] * square_diag[0:1, s]
-            b0[:, s] = value
-            h2[:, s] = (value + y_of(s) * diags[0:1, s]).astype(bf16)
-
-        times(h0, near, finish_4)
-
-        def finish_5(s, value):
-            fourth, mix = b0[:, s], y_of(s)
-            fifth = value + 1.25 * (fourth + mix * diags[0:1, s])
-            value = 1.25 * (mix - fourth) + fifth + mix * diags[1:2, s]
-            b1[:, s] = value
-            h0[:, s] = value.astype(bf16)
-
-        times(h2, near, finish_5)
-
-        def finish_6(s, value):
-            b0[:, s] = value + 1.25 * b1[:, s] + y_of(s) * diags[2:3, s]
-
-        times(h0, near, finish_6)
-
-        def squares(k, total):
-            value = b0[:, at(k * LANES, LANES)]
-            return total + fold(value * value)
-
-        partial = lax.fori_loop(0, N // LANES, squares, jnp.zeros((8, LANES), f32))
-        totals[0] = partial
-        copies = []
-        for k, peer in enumerate(peers):
-            copies.append(
-                pltpu.make_async_remote_copy(
-                    src_ref=totals.at[0],
-                    dst_ref=totals.at[k + 1],
-                    send_sem=total_send.at[k],
-                    recv_sem=total_recv.at[k],
-                    device_id=peer,
-                    device_id_type=MESH,
-                )
-            )
-        for copy in copies:
-            copy.start()
-        for copy in copies:
+        diags_copy.start()
+        for copy in factor_keeps():
             copy.wait()
-        total = totals[0]
-        for k in range(1, 8):
-            total = total + totals[k]
-        upd = jnp.sum(jnp.sum(total, axis=0, keepdims=True), axis=1, keepdims=True)
-        factor = jnp.sqrt(trace / (N * N)) * lax.rsqrt(upd / (N * N) + graft_floor)
-
-        def scaled(k, _):
-            s = at(k * TILE, TILE)
-            h0[:, s] = (b0[:, s] * factor).astype(bf16)
-            return 0
-
-        lax.fori_loop(0, N // TILE, scaled, 0)
-        result_copy().start()
-        keep = pltpu.make_async_copy(h0.at[HALF:TILE], update.at[0], local_sem.at[0])
-        keep.start()
-        keep.wait()
-        result_copy().wait_send()
+        mixed_copy.wait_recv()
+
+    top = slice(0, HALF)
+    b0, b1, h0, h2 = b0.at[top], b1.at[top], h0.at[top], h1.at[top]
+
+    def y_of(s):
+        return mixed[:, s].astype(f32)
+
+    def finish_1(s, value):
+        value = value + 1.25 * y_of(s)
+        b0[:, s] = value
+        h0[:, s] = value.astype(bf16)
+
+    times(mixed, other, finish_1)
+
+    def finish_2(s, value):
+        value = value + 1.25 * b0[:, s] + y_of(s) * square_right[0:1, s]
+        b1[:, s] = value
+        h2[:, s] = value.astype(bf16)
+
+    times(h0, other, finish_2)
+
+    def finish_3(s, value):
+        value = value + 1.25 * b1[:, s]
+        b0[:, s] = value
+        h0[:, s] = value.astype(bf16)
+
+    times(h2, other, finish_3)
+
+    @pl.when(core == 0)
+    def _():
+        diags_copy.wait_recv()
+
+    def finish_4(s, value):
+        value = value + 1.25 * b0[:, s] + b1[:, s] * square_right[0:1, s]
+        b0[:, s] = value
+        h2[:, s] = (value + y_of(s) * diags[0:1, s]).astype(bf16)
+
+    times(h0, other, finish_4)
+
+    def finish_5(s, value):
+        fourth, mix = b0[:, s], y_of(s)
+        fifth = value + 1.25 * (fourth + mix * diags[0:1, s])
+        value = 1.25 * (mix - fourth) + fifth + mix * diags[1:2, s]
+        b1[:, s] = value
+        h0[:, s] = value.astype(bf16)
+
+    times(h2, other, finish_5)
+
+    def finish_6(s, value):
+        result[:, s] = value + 1.25 * b1[:, s] + y_of(s) * diags[2:3, s]
+
+    times(h0, other, finish_6)
+
+    def squares(k, total):
+        value = result[:, at(k * LANES, LANES)]
+        return total + fold(value * value)
+
+    totals[0] = lax.fori_loop(0, N // LANES, squares, jnp.zeros((8, LANES), f32))
+    copy = remote(
+        totals.at[0], totals.at[8], total_send.at[7], total_recv.at[7], {"grp": sibling}
+    )
+    copy.start()
+    copy.wait()
+    totals[9] = totals[0] + totals[8]
+    copies = [
+        remote(totals.at[9], totals.at[k + 1], total_send.at[k], total_recv.at[k], peer)
+        for k, peer in enumerate(peers)
+    ]
+    for copy in copies:
+        copy.start()
+    for copy in copies:
+        copy.wait()
+    total = totals[9]
+    for k in range(1, 8):
+        total = total + totals[k]
+    upd = jnp.sum(jnp.sum(total, axis=0, keepdims=True), axis=1, keepdims=True)
+    value = jnp.sqrt(trace / (N * N)) * lax.rsqrt(upd / (N * N) + graft_floor)
+    update[0] = (result[...] * value).astype(bf16)
+
+    @pl.when(core == 0)
+    def _():
+        mixed_copy.wait_send()
+
+    @pl.when(core == 1)
+    def _():
+        diags_copy.wait_send()
+        for copy in factor_copies():
+            copy.wait_send()
 
 
 def refresh(grad):
@@ -605,42 +652,45 @@
         refresh_kernel,
         out_shape=jax.ShapeDtypeStruct((1, HALF, N), bf16),
         in_specs=[pl.BlockSpec(memory_space=pl.ANY)],
-        out_specs=pl.BlockSpec(memory_space=pl.ANY),
+        out_specs=pl.BlockSpec(memory_space=pltpu.VMEM),
         scratch_shapes=[
             pltpu.VMEM((N, N), bf16),
             pltpu.VMEM((N, N), bf16),
+            pltpu.VMEM((N, N), bf16),
             pltpu.VMEM((N, N), f32),
-            pltpu.VMEM((8, 64, 512), bf16),
+            pltpu.VMEM((UNITS, SHARE, 512), bf16),
             pltpu.VMEM((TILE, LANES), f32),
             pltpu.VMEM((TILE, N), bf16),
             pltpu.VMEM((TILE, N), bf16),
             pltpu.VMEM((TILE, N), bf16),
             pltpu.VMEM((TILE, N), bf16),
+            pltpu.VMEM((HALF, N), bf16),
+            pltpu.VMEM((8, N), f32),
             pltpu.VMEM((8, N), f32),
             pltpu.VMEM((2, 8, LANES), f32),
             pltpu.VMEM((8, N), f32),
-            pltpu.VMEM((8, 8, LANES), f32),
-            dma((2,)),
-            dma((2, 8)),
-            dma((2, 8)),
-            dma((3, 8)),
-            dma((3, 8)),
-            dma((2, 8)),
-            dma((2, 8)),
-            dma((3, 8)),
-            dma((3, 8)),
-            dma((2,)),
+            pltpu.VMEM((HALF, N), f32),
+            pltpu.VMEM((10, 8, LANES), f32),
+            dma((2, SPLIT)),
+            dma((2, UNITS)),
+            dma((2, UNITS)),
+            dma((3, UNITS)),
+            dma((3, UNITS)),
+            dma((2, UNITS)),
+            dma((2, UNITS)),
+            dma((3, UNITS)),
+            dma((3, UNITS)),
+            dma((6,)),
+            dma((4,)),
             dma((7, 2)),
             dma((7, 2)),
-            dma((7,)),
-            dma((7,)),
-            dma((2,)),
+            dma((8,)),
+            dma((8,)),
         ],
         compiler_params=pltpu.CompilerParams(
             collective_id=0, has_side_effects=True, vmem_limit_bytes=62 * 1024 * 1024
         ),
     )(grad)
-
 
 def solution(mesh):
     return jax.shard_map(

time: 126 us -> 114 us (0.905)
  Pallas kernels: 124 us -> 112 us
    pallas_call x1, Pallas kernels: 124 us -> 112 us  [refresh(): pl.pallas_call(refresh_kernel, out_shape=jax.ShapeDtypeStruct((1, HALF, N...]
where the time goes in v3:
time: 114 us
  Pallas kernels  112 us (98%)
  local copies, waits for them, and re-layouts  1.88 us (2%)
    pallas_call x1, Pallas kernels, refresh(): pl.pallas_call(refresh_kernel, out_shape=jax.ShapeDtypeStruct((1, HALF, N...  112 us

profile of v3, /device:TPU:1, one launch (start us, length us, event | category | flops | bytes accessed | tf_op | source)
XLA Modules:
  0.0 113.5 jit_solution(17560547670144419068)
XLA Ops:
  0.0 111.6 %shard_map.17 = bf16[1,128,2048]{2,1,0:T(8,128)(2,1)} custom-call(bf16[16,64,2048]{2,1,0:T(8,128)(2,1)} %grad.1), custom_call_target="tpu_custom_call" | custom-call | tf_op jit(solution)/shard_map/pallas_call | solution.py:651
  111.6 1.9 %copy.3 = bf16[1,128,2048]{2,1,0:T(8,128)(2,1)} copy(bf16[1,128,2048]{2,1,0:T(8,128)(2,1)} %shard_map.17) | data formatting | bytes 1048576

commit v4 on v3

--- a/solution.py
+++ b/solution.py
@@ -104,13 +104,14 @@
 
 
 def add_diagonal(stat, value):
-    def step(i, trace):
-        where = (at(i * TILE, TILE), at(i * TILE, TILE))
-        old, mask = stat[where], eye(TILE)
+    trace = jnp.zeros((8, LANES), f32)
+    mask = eye(LANES)
+    for k in range(N // LANES):
+        where = (slice(k * LANES, (k + 1) * LANES),) * 2
+        old = stat[where]
         stat[where] = jnp.where(mask, old + value, old)
-        return trace + jnp.sum(jnp.where(mask, old, 0.0), keepdims=True)
-
-    return lax.fori_loop(0, 8, step, jnp.zeros((1, 1), f32))
+        trace = trace + fold(jnp.where(mask, old, 0.0))
+    return jnp.sum(jnp.sum(trace, axis=0, keepdims=True), axis=1, keepdims=True)
 
 
 def fold(value):
@@ -121,47 +122,50 @@
     return total
 
 
-def power(stat, rows=128):
+def power(stat, images, rows=512, part=64):
     count = N // LANES
     blocks = N // rows
-
-    def images(i, vector):
-        where = at(i * rows, rows)
-        total = None
-        for k in range(count):
-            part = stat[where, k * LANES : (k + 1) * LANES].reshape(rows // 8, 8, LANES)
-            part = part * vector[k][None]
-            total = part if total is None else total + part
-        total = jnp.sum(total.reshape(rows, LANES), axis=1, keepdims=True)
-        return jnp.broadcast_to(total, (rows, LANES))
-
-    def shares(i, image, sums):
-        where = at(i * rows, rows)
-        return tuple(
-            sums[k] + fold(stat[where, k * LANES : (k + 1) * LANES] * image)
-            for k in range(count)
-        )
+    ones = jnp.ones((LANES, LANES), bf16)
+
+    def column(k):
+        return slice(k * LANES, (k + 1) * LANES)
+
+    def image(i, vector):
+        for p in range(rows // part):
+            where = at(i * rows + p * part, part)
+            total = None
+            for k in range(count):
+                value = stat[where, column(k)].reshape(part // 8, 8, LANES) * vector[k][None]
+                total = value if total is None else total + value
+            total = total.reshape(part, LANES)
+            high = total.astype(bf16)
+            low = (total - high.astype(f32)).astype(bf16)
+            images[where, :] = jnp.dot(
+                high, ones, preferred_element_type=f32
+            ) + jnp.dot(low, ones, preferred_element_type=f32)
+
+    def share(i, sums, squares):
+        sums = list(sums)
+        for p in range(rows // part):
+            where = at(i * rows + p * part, part)
+            entries = images[where, :]
+            squares = squares + fold(entries * entries)
+            for k in range(count):
+                sums[k] = sums[k] + fold(stat[where, column(k)] * entries)
+        return tuple(sums), squares
 
     def double(_, carry):
         vector, _norm = carry
+        image(0, vector)
 
         def body(i, state):
-            image, sums, squares = state
-            later = images(i + 1, vector)
-            return later, shares(i, image, sums), squares + image * image
-
-        image, sums, squares = lax.fori_loop(
-            0,
-            blocks - 1,
-            body,
-            (
-                images(0, vector),
-                tuple(jnp.zeros((8, LANES), f32) for _ in range(count)),
-                jnp.zeros((rows, LANES), f32),
-            ),
-        )
-        sums = shares(blocks - 1, image, sums)
-        first = jnp.sum(squares + image * image, axis=0, keepdims=True)[:, 0:1]
+            image(i + 1, vector)
+            return share(i, *state)
+
+        zero = jnp.zeros((8, LANES), f32)
+        state = lax.fori_loop(0, blocks - 1, body, ((zero,) * count, zero))
+        sums, squares = share(blocks - 1, *state)
+        first = jnp.sum(squares, axis=0, keepdims=True)[:, 0:1]
         result = [jnp.sum(s, axis=0, keepdims=True) for s in sums]
         square = result[0] * result[0]
         for k in range(1, count):
@@ -224,6 +228,7 @@
     other,
     stat,
     staging,
+    images,
     wide,
     rows_near,
     h0,
@@ -411,7 +416,7 @@
     regions = (region(4 * y + side), region(4 * y + side + 2))
 
     trace = add_diagonal(stat, N * damping)
-    norm = power(stat)
+    norm = power(stat, images)
     square = build(stat, norm, near)
     b0, b1 = stat.at[0:TILE], stat.at[TILE : 2 * TILE]
     for k in range(N // LANES):
@@ -659,6 +664,7 @@
             pltpu.VMEM((N, N), bf16),
             pltpu.VMEM((N, N), f32),
             pltpu.VMEM((UNITS, SHARE, 512), bf16),
+            pltpu.VMEM((N, LANES), f32),
             pltpu.VMEM((TILE, LANES), f32),
             pltpu.VMEM((TILE, N), bf16),
             pltpu.VMEM((TILE, N), bf16),

time: 114 us -> 111 us (0.974)
  Pallas kernels: 112 us -> 109 us
    pallas_call x1, Pallas kernels: 112 us -> 109 us  [refresh(): pl.pallas_call(refresh_kernel, out_shape=jax.ShapeDtypeStruct((1, HALF, N...]
where the time goes in v4:
time: 111 us
  Pallas kernels  109 us (98%)
  local copies, waits for them, and re-layouts  1.88 us (2%)
    pallas_call x1, Pallas kernels, refresh(): pl.pallas_call(refresh_kernel, out_shape=jax.ShapeDtypeStruct((1, HALF, N...  109 us

profile of v4, /device:TPU:1, one launch (start us, length us, event | category | flops | bytes accessed | tf_op | source)
XLA Modules:
  0.0 110.8 jit_solution(15435613239503968466)
XLA Ops:
  0.0 109.0 %shard_map.17 = bf16[1,128,2048]{2,1,0:T(8,128)(2,1)} custom-call(bf16[16,64,2048]{2,1,0:T(8,128)(2,1)} %grad.1), custom_call_target="tpu_custom_call" | custom-call | tf_op jit(solution)/shard_map/pallas_call | solution.py:656
  109.0 1.9 %copy.3 = bf16[1,128,2048]{2,1,0:T(8,128)(2,1)} copy(bf16[1,128,2048]{2,1,0:T(8,128)(2,1)} %shard_map.17) | data formatting | bytes 1048576
